TPU v7x, 128 devices: a whole 4x4x4 slice. The times are simulated.
128 devices in a mesh: ctx: 16 (over x, y_hi, core), tp: 8 (over y_lo, z).
Axes of the slice: x: 4, y: 4 (y_hi: 2, y_lo: 2; y = y_hi * 2 + y_lo), z: 4, core: 2. Of those that a mesh axis runs over, the one named last changes fastest.
Arguments:
- queries: bfloat16 [2048, 16384], P('ctx', 'tp'), may hold values from -48 to 48
- cache_keys: bfloat16 [16384, 1024], P('ctx', 'tp'), may hold values from -6.4 to 6.4
- cache_values: bfloat16 [16384, 1024], P('ctx', 'tp'), may hold values from -6 to 6
- new_keys: bfloat16 [2048, 1024], P(('ctx', 'tp')), may hold values from -6.375 to 6.375
- new_values: bfloat16 [2048, 1024], P(('ctx', 'tp')), may hold values from -6 to 6
- sources: int32 [2048], replicated, may hold values from 0 to 2047, each once
Outputs:
- attended: bfloat16 [2048, 16384], P('ctx', 'tp')
Inputs may be any that keep to these rules, and one draw needn't show every extreme that they name: `sources`: every new token appears once; append slot s belongs to owner s // 128.
All inputs are finite; a program needn't handle non-finite values.
Results may differ from a plain program's by a relative error of at most 0.0015.
The roundings to bfloat16 on the way count: a program that leaves them out, or rounds other values in their place, can miss the bound.
Values may be sent and summed in bfloat16 or wider, within the bound.
A program may use at most 128 MiB of HBM per device.

v0:
```python
import functools
import math

import jax
import jax.numpy as jnp
from jax import lax
from jax.experimental import pallas as pl
from jax.experimental.pallas import tpu as pltpu
from jax.sharding import PartitionSpec as P

HEAD_DIM = 128
GROUP = 16
OWNERS = 16
TP = 8
NEW = 128
CACHE = 1024
KEYS = CACHE + NEW
ROWS = NEW * GROUP
TILE = 1024
TILES = ROWS // TILE
WIDE = 256
SPLITS = TILE // WIDE
MASKED = -1e30
SCALE = math.log2(math.e) / math.sqrt(HEAD_DIM)
MESH = pl.DeviceIdType.MESH
NT = (((1,), (1,)), ((), ()))
f32, bf16 = jnp.float32, jnp.bfloat16

CHIPS = [(0, 0), (-1, 0), (1, 0), (2, 0), (0, 1), (-1, 1), (1, 1), (2, 1)]
GROUP_OF = {chip: i for i, chip in enumerate(CHIPS)}


def kernel(
    q_ref, ck_ref, cv_ref, nk_ref, nv_ref, src_ref, o_ref,
    kc, vc, newt, kn, vn, lim, hot, vtmp, pack, stage, q2, sb, mb, pb, lb, mm, acc, den, top,
    local_sem, p1_send, p1_recv, p2_send, p2_recv, k_send, k_recv, v_send, v_recv,
):
    ctx, tp = lax.axis_index("ctx"), lax.axis_index("tp")
    x, yh, core = ctx // 4, (ctx // 2) % 2, ctx % 2

    def owner_at(dx, dy, dc):
        return ((x + dx + 4) % 4) * 4 + ((yh + dy) % 2) * 2 + (core + dc) % 2

    def owner_of(slot):
        group = slot // 2
        place = group % 4
        dx = (3 * place + (place // 2) * (2 * place - 5)) % 4
        return owner_at(dx, group // 4, slot % 2)

    sibling = (owner_at(0, 0, 1), tp)
    right = (owner_at(1, 0, 0), tp)
    left = (owner_at(-1, 0, 0), tp)
    across = (owner_at(0, 1, 0), tp)

    def remote(src, dst, send, recv, to):
        return pltpu.make_async_remote_copy(
            src_ref=src, dst_ref=dst, send_sem=send, recv_sem=recv, device_id=to, device_id_type=MESH
        )

    def carrier(buf, send, recv):
        def go(at, src, dst, to):
            remote(buf.at[src], buf.at[dst], send.at[at], recv.at[dst], to).start()

        def landed(slot):
            pltpu.make_async_copy(buf.at[slot], buf.at[slot], recv.at[slot]).wait()

        def gone(at):
            pltpu.make_async_copy(buf.at[0], buf.at[0], send.at[at]).wait()

        return go, landed, gone

    go_k, landed_k, gone_k = carrier(kc, k_send, k_recv)
    go_v, landed_v, gone_v = carrier(vc, v_send, v_recv)
    go_n, landed_n, gone_n = carrier(newt, p2_send, p2_recv)

    barrier = pltpu.get_barrier_semaphore()
    peers = [(ctx, (tp + d) % TP) for d in range(1, TP)]
    peers += [(owner_at(dx, dy, 0), tp) for dx, dy in CHIPS[1:]] + [sibling]
    for peer in peers:
        pl.semaphore_signal(barrier, inc=1, device_id=peer, device_id_type=MESH)

    own_k = pltpu.make_async_copy(ck_ref, kc.at[0], local_sem.at[0])
    own_v = pltpu.make_async_copy(cv_ref, vtmp, local_sem.at[1])
    own_k.start()
    own_v.start()
    for h in range(TP):
        cols = slice(h * HEAD_DIM, (h + 1) * HEAD_DIM)
        pack[h, :16, :] = nk_ref[:, cols]
        pack[h, 16:, :] = nv_ref[:, cols]
    stage[tp] = pack[tp]
    own_k.wait()

    pl.semaphore_wait(barrier, len(peers))
    for d in range(1, TP):
        head = (tp + d) % TP
        remote(pack.at[head], stage.at[tp], p1_send.at[d - 1], p1_recv.at[d - 1], (ctx, head)).start()
    go_k(0, 0, 1, sibling)
    go_k(1, 0, 2, right)
    go_k(2, 0, 4, left)

    for h in range(GROUP):
        rows = pl.ds(h * NEW, NEW)
        part = q_ref[:, pl.ds(h * HEAD_DIM, HEAD_DIM)].astype(f32) * SCALE
        high = part.astype(bf16)
        q2[rows, :HEAD_DIM] = high
        q2[rows, HEAD_DIM:] = (part - high.astype(f32)).astype(bf16)
    own_v.wait()
    for b in range(CACHE // 128):
        vc[0, :, b * 128 : (b + 1) * 128] = vtmp[b * 128 : (b + 1) * 128, :].astype(f32).T.astype(bf16)
    go_v(0, 0, 1, sibling)
    acc[...] = jnp.zeros_like(acc)
    den[...] = jnp.zeros_like(den)
    top[...] = jnp.full_like(top, MASKED)

    def limits(slot, carry):
        owner = owner_of(slot)
        pos = jnp.broadcast_to(src_ref[pl.ds(owner, 1), :].astype(f32), (NEW, NEW)).T
        token = (ctx * NEW + lax.broadcasted_iota(jnp.int32, (NEW, NEW), 1)).astype(f32)
        lim[slot] = jnp.where(pos <= token, f32(3e38), f32(MASKED))
        return carry

    lax.fori_loop(0, OWNERS, limits, 0)

    def columns(c):
        return pl.ds(c * WIDE, WIDE)

    def scores(keys, j, c):
        queries = q2[pl.ds(pl.multiple_of(j * TILE + c * WIDE, WIDE), WIDE), :]
        return lax.dot_general(
            jnp.concatenate([keys, keys], axis=1), queries, NT, preferred_element_type=f32
        )

    def peaks(s):
        return jnp.max(s.reshape(s.shape[0] // 8, 8, WIDE), axis=0)

    def masked(s, slot):
        return jnp.minimum(s, jnp.concatenate([lim[slot]] * (WIDE // NEW), axis=1))

    def score(slot, j, c):
        s = scores(jnp.concatenate([kc[slot], kn[slot]], axis=0), j, c)
        cached, new = s[:CACHE], masked(s[CACHE:], slot)
        sb[:CACHE, columns(c)] = cached
        sb[CACHE:, columns(c)] = new
        mb[:, columns(c)] = jnp.maximum(peaks(cached), peaks(new))

    def weigh(c):
        cols = columns(c)
        peak = jnp.max(mb[:, cols], axis=0, keepdims=True)
        total = None
        for at in range(0, KEYS, 128):
            w = jnp.exp2(sb[at : at + 128, cols] - peak)
            part = jnp.sum(w.reshape(16, 8, WIDE), axis=0)
            total = part if total is None else total + part
            pb[at : at + 128, cols] = w.astype(bf16)
        lb[:, cols] = jnp.sum(total, axis=0, keepdims=True)
        mm[:, cols] = peak

    def mix(slot, j, c):
        cols = columns(c)
        total, peak = lb[:, cols], mm[:, cols]
        values = jnp.concatenate([vc[slot], vn[slot]], axis=1)
        mixed = jnp.dot(values, pb[:, cols], preferred_element_type=f32)
        partial = (mixed * (1.0 / total)).astype(bf16).astype(f32)
        lse = peak + jnp.log2(total)
        old = top[j, :, cols]
        new = jnp.maximum(old, lse)
        keep, add = jnp.exp2(old - new), jnp.exp2(lse - new)
        acc[j, :, cols] = acc[j, :, cols] * keep + partial * add
        den[j, :, cols] = den[j, :, cols] * keep + add
        top[j, :, cols] = new

    for c in range(SPLITS):
        s = scores(kc[0], 0, c)
        sb[:CACHE, columns(c)] = s
        mb[:, columns(c)] = peaks(s)

    for d in range(1, TP):
        source = (tp - d + TP) % TP
        pltpu.make_async_copy(stage.at[source], stage.at[source], p1_recv.at[d - 1]).wait()
    for i in range(2):
        rows = jnp.concatenate([stage[h, i * 16 : (i + 1) * 16, :] for h in range(TP)], axis=0)
        newt[0, i * HEAD_DIM : (i + 1) * HEAD_DIM, :] = rows.astype(f32).T.astype(bf16)
    for g in (4, 7, 5, 6, 3, 1, 2):
        dx, dy = CHIPS[g]
        back = GROUP_OF[(-dx if abs(dx) == 1 else dx, dy)]
        go_n(g, 0, 2 * back, (owner_at(dx, dy, 0), tp))
    go_n(0, 0, 1, sibling)
    go_v(1, 0, 2, right)
    go_v(2, 0, 4, left)
    go_k(3, 0, 8, across)

    def choose(pair, carry):
        want = jnp.concatenate(
            [src_ref[pl.ds(owner_of(2 * pair + i), 1), :] for i in range(2)], axis=1
        )
        for slot in range(OWNERS):
            dx, dy = CHIPS[slot // 2]
            token = owner_at(dx, dy, slot % 2) * NEW + lax.broadcasted_iota(jnp.int32, (NEW, 2 * NEW), 0)
            rows = slice(slot * NEW, (slot + 1) * NEW)
            hot[pair, rows, :] = jnp.where(token == want, f32(1), f32(0)).astype(bf16)
        return carry

    lax.fori_loop(0, OWNERS // 2, choose, 0)

    for g in (1, 2, 3, 4, 5, 6, 7):
        landed_n(2 * g)
        go_n(7 + g, 2 * g, 2 * g + 1, sibling)
    go_v(3, 0, 8, across)
    landed_k(2)
    go_k(4, 2, 6, right)
    go_k(5, 2, 3, sibling)
    landed_k(4)
    go_k(6, 4, 5, sibling)
    landed_n(1)
    for g in range(1, 8):
        landed_n(2 * g + 1)

    def pick(pair):
        rows = jnp.concatenate([newt[slot] for slot in range(OWNERS)], axis=1)
        got = jnp.dot(rows, hot[pair], preferred_element_type=f32)
        for i in range(2):
            cols = slice(i * NEW, (i + 1) * NEW)
            kn[2 * pair + i] = got[:HEAD_DIM, cols].T.astype(bf16)
            vn[2 * pair + i] = got[HEAD_DIM:, cols].astype(bf16)

    pick(0)
    for c in range(SPLITS):
        s = masked(scores(kn[0], 0, c), 0)
        sb[CACHE:, columns(c)] = s
        mb[:, columns(c)] = jnp.maximum(mb[:, columns(c)], peaks(s))
    for i in range(SPLITS + 1):
        if i >= 1:
            score(0, 1, i - 1)
        if i < SPLITS:
            weigh(i)

    def relay(slot):
        @pl.when(slot % 2 == 1)
        def _():
            pick((slot + 1) // 2)

        @pl.when(slot == 0)
        def _():
            landed_k(1)
            landed_v(1)

        @pl.when(slot == 1)
        def _():
            landed_v(2)
            go_v(4, 2, 3, sibling)
            landed_v(4)
            go_v(5, 4, 6, left)
            go_v(6, 4, 5, sibling)
            landed_k(8)
            go_k(7, 8, 10, right)
            go_k(8, 8, 12, left)
            go_k(9, 8, 9, sibling)

        @pl.when(slot == 2)
        def _():
            landed_k(3)

        @pl.when(slot == 3)
        def _():
            landed_v(3)
            landed_k(6)
            go_k(10, 6, 14, across)
            go_k(11, 6, 7, sibling)
            landed_v(8)
            go_v(7, 8, 10, right)
            go_v(8, 8, 12, left)
            go_v(9, 8, 9, sibling)

        @pl.when(slot == 4)
        def _():
            landed_k(5)
            landed_v(5)
            landed_v(6)
            go_v(10, 6, 14, across)
            go_v(11, 6, 7, sibling)

        @pl.when(slot == 6)
        def _():
            landed_k(7)
            landed_v(7)
            landed_k(10)
            go_k(12, 10, 11, sibling)
            landed_k(12)
            go_k(13, 12, 13, sibling)

        @pl.when(slot == 8)
        def _():
            landed_k(9)
            landed_v(9)
            landed_v(10)
            go_v(12, 10, 11, sibling)
            landed_v(12)
            go_v(13, 12, 13, sibling)
            landed_k(14)
            go_k(14, 14, 15, sibling)
            landed_v(14)
            go_v(14, 14, 15, sibling)

        @pl.when(slot == 10)
        def _():
            landed_k(11)
            landed_v(11)

        @pl.when(slot == 12)
        def _():
            landed_k(13)
            landed_v(13)

        @pl.when(slot == 14)
        def _():
            landed_k(15)
            landed_v(15)

    def owner_step(slot, carry):
        relay(slot)

        def step(j, carry):
            for i in range(SPLITS + 2):
                if i >= 2:
                    score(slot + 1, j, i - 2)
                if 1 <= i <= SPLITS:
                    weigh(i - 1)
                if i < SPLITS:
                    mix(slot, j, i)
            return carry

        return lax.fori_loop(0, TILES, step, carry)

    lax.fori_loop(0, OWNERS - 1, owner_step, 0)
    for i in range(SPLITS + 1):
        if i >= 1:
            weigh(i - 1)
        if i < SPLITS:
            mix(OWNERS - 1, TILES - 2, i)
    for c in range(SPLITS):
        mix(OWNERS - 1, TILES - 1, c)

    per = TILE // NEW
    for h in range(GROUP):
        j, at = h // per, (h % per) * NEW
        part = acc[j, :, at : at + NEW] * (1.0 / den[j, :, at : at + NEW])
        o_ref[:, h * HEAD_DIM : (h + 1) * HEAD_DIM] = part.T.astype(bf16)

    for d in range(1, TP):
        pltpu.make_async_copy(pack.at[0], pack.at[0], p1_send.at[d - 1]).wait()
    for at in range(15):
        gone_n(at)
        gone_k(at)
        gone_v(at)


def on_device(queries, cache_keys, cache_values, new_keys, new_values, sources):
    vmem, dma = pltpu.VMEM, pltpu.SemaphoreType.DMA
    whole = pl.BlockSpec(memory_space=pltpu.VMEM)
    there = pl.BlockSpec(memory_space=pl.ANY)
    return pl.pallas_call(
        kernel,
        out_shape=jax.ShapeDtypeStruct(queries.shape, queries.dtype),
        in_specs=[whole, there, there, whole, whole, whole],
        out_specs=whole,
        scratch_shapes=[
            vmem((OWNERS, CACHE, HEAD_DIM), bf16),
            vmem((OWNERS, HEAD_DIM, CACHE), bf16),
            vmem((OWNERS, 2 * HEAD_DIM, NEW), bf16),
            vmem((OWNERS, NEW, HEAD_DIM), bf16),
            vmem((OWNERS, HEAD_DIM, NEW), bf16),
            vmem((OWNERS, NEW, NEW), f32),
            vmem((OWNERS // 2, OWNERS * NEW, 2 * NEW), bf16),
            vmem((CACHE, HEAD_DIM), bf16),
            vmem((TP, 32, HEAD_DIM), bf16),
            vmem((TP, 32, HEAD_DIM), bf16),
            vmem((ROWS, 2 * HEAD_DIM), bf16),
            vmem((KEYS, TILE), f32),
            vmem((8, TILE), f32),
            vmem((KEYS, TILE), bf16),
            vmem((1, TILE), f32),
            vmem((1, TILE), f32),
            vmem((TILES, HEAD_DIM, TILE), f32),
            vmem((TILES, 1, TILE), f32),
            vmem((TILES, 1, TILE), f32),
            dma((2,)),
            dma((7,)),
            dma((7,)),
            dma((15,)),
            dma((OWNERS,)),
            dma((15,)),
            dma((OWNERS,)),
            dma((15,)),
            dma((OWNERS,)),
        ],
        compiler_params=pltpu.CompilerParams(
            collective_id=0, has_side_effects=True, vmem_limit_bytes=60 * 2**20
        ),
    )(queries, cache_keys, cache_values, new_keys, new_values, sources.reshape(OWNERS, NEW))


def solution(mesh):
    placed = (
        P("ctx", "tp"),
        P("ctx", "tp"),
        P("ctx", "tp"),
        P(("ctx", "tp"), None),
        P(("ctx", "tp"), None),
        P(),
    )
    return jax.shard_map(on_device, mesh=mesh, in_specs=placed, out_specs=P("ctx", "tp"), check_vma=False)
```

profile of v0, /device:TPU:1, one launch (start us, length us, event | category | flops | bytes accessed | tf_op | source)
XLA Modules:
  0.0 75.3 jit_solution(12143038968776026091)
XLA Ops:
  0.0 73.4 %shard_map.64 = bf16[128,2048]{1,0:T(8,128)(2,1)} custom-call(bf16[128,2048]{1,0:T(8,128)(2,1)} %q_ref.1, bf16[1024,128]{1,0:T(8,128)(2,1)} %ck_ref.1, bf16[1024,128]{1,0:T(8,128)(2,1)} %cv_ref.1, bf16[16,1024]{1,0:T(8,128)(2,1)} %nk_ref.1, bf16[16,1024]{1,0:T(8,128)(2,1)} %nv_ref.1, s32[16,128]{1,0:T(8,128)} %bitcast.1), custom_call_target="tpu_custom_call" | custom-call | tf_op jit(solution)/shard_map/pallas_call | solution.py:361
  73.4 1.9 %copy.8 = bf16[128,2048]{1,0:T(8,128)(2,1)} copy(bf16[128,2048]{1,0:T(8,128)(2,1)} %shard_map.64) | data formatting | bytes 1048576
where the time goes:
time: 75.5 us; the launch traced here: 75.3 us
  Pallas kernels  73.4 us (97%)
  local copies, waits for them, and re-layouts  1.88 us (2%)
    pallas_call x1, Pallas kernels, on_device(): pl.pallas_call(kernel, out_shape=jax.ShapeDtypeStruct(queries.shape, quer...  73.4 us
    unnamed x1, local copies, waits for them, and re-layouts  1.88 us

commit v1 on v0

--- a/solution.py
+++ b/solution.py
@@ -20,6 +20,7 @@
 TILES = ROWS // TILE
 WIDE = 256
 SPLITS = TILE // WIDE
+AHEAD = 4
 MASKED = -1e30
 SCALE = math.log2(math.e) / math.sqrt(HEAD_DIM)
 MESH = pl.DeviceIdType.MESH
@@ -32,8 +33,8 @@
 
 def kernel(
     q_ref, ck_ref, cv_ref, nk_ref, nv_ref, src_ref, o_ref,
-    kc, vc, newt, kn, vn, lim, hot, vtmp, pack, stage, q2, sb, mb, pb, lb, mm, acc, den, top,
-    local_sem, p1_send, p1_recv, p2_send, p2_recv, k_send, k_recv, v_send, v_recv,
+    kc, vc, newk, newv, kn, vn, lim, hot, vtmp, pack, stage, q2, sa, ma, sb, mb, pb, lb, mm, acc, den, top,
+    local_sem, p1_send, p1_recv, nk_send, nk_recv, nv_send, nv_recv, k_send, k_recv, v_send, v_recv,
 ):
     ctx, tp = lax.axis_index("ctx"), lax.axis_index("tp")
     x, yh, core = ctx // 4, (ctx // 2) % 2, ctx % 2
@@ -71,7 +72,8 @@
 
     go_k, landed_k, gone_k = carrier(kc, k_send, k_recv)
     go_v, landed_v, gone_v = carrier(vc, v_send, v_recv)
-    go_n, landed_n, gone_n = carrier(newt, p2_send, p2_recv)
+    go_nk, landed_nk, gone_nk = carrier(newk, nk_send, nk_recv)
+    go_nv, landed_nv, gone_nv = carrier(newv, nv_send, nv_recv)
 
     barrier = pltpu.get_barrier_semaphore()
     peers = [(ctx, (tp + d) % TP) for d in range(1, TP)]
@@ -143,12 +145,16 @@
         sb[CACHE:, columns(c)] = new
         mb[:, columns(c)] = jnp.maximum(peaks(cached), peaks(new))
 
-    def weigh(c):
+    def weigh(c, ahead=None):
         cols = columns(c)
         peak = jnp.max(mb[:, cols], axis=0, keepdims=True)
         total = None
         for at in range(0, KEYS, 128):
-            w = jnp.exp2(sb[at : at + 128, cols] - peak)
+            if ahead is None or at >= CACHE:
+                s = sb[at : at + 128, cols]
+            else:
+                s = sa[ahead, at : at + 128, cols]
+            w = jnp.exp2(s - peak)
             part = jnp.sum(w.reshape(16, 8, WIDE), axis=0)
             total = part if total is None else total + part
             pb[at : at + 128, cols] = w.astype(bf16)
@@ -169,25 +175,34 @@
         den[j, :, cols] = den[j, :, cols] * keep + add
         top[j, :, cols] = new
 
-    for c in range(SPLITS):
-        s = scores(kc[0], 0, c)
-        sb[:CACHE, columns(c)] = s
-        mb[:, columns(c)] = peaks(s)
+    def score_cached(slot, j, ahead):
+        for c in range(SPLITS):
+            s = scores(kc[slot], j, c)
+            sa[ahead, :, columns(c)] = s
+            ma[ahead, :, columns(c)] = peaks(s)
+
+    def score_new(slot, j, ahead, c):
+        s = masked(scores(kn[slot], j, c), slot)
+        sb[CACHE:, columns(c)] = s
+        mb[:, columns(c)] = jnp.maximum(ma[ahead, :, columns(c)], peaks(s))
+
+    score_cached(0, 0, 0)
 
     for d in range(1, TP):
         source = (tp - d + TP) % TP
         pltpu.make_async_copy(stage.at[source], stage.at[source], p1_recv.at[d - 1]).wait()
-    for i in range(2):
+    for i, (new, go) in enumerate(((newk, go_nk), (newv, go_nv))):
         rows = jnp.concatenate([stage[h, i * 16 : (i + 1) * 16, :] for h in range(TP)], axis=0)
-        newt[0, i * HEAD_DIM : (i + 1) * HEAD_DIM, :] = rows.astype(f32).T.astype(bf16)
-    for g in (4, 7, 5, 6, 3, 1, 2):
-        dx, dy = CHIPS[g]
-        back = GROUP_OF[(-dx if abs(dx) == 1 else dx, dy)]
-        go_n(g, 0, 2 * back, (owner_at(dx, dy, 0), tp))
-    go_n(0, 0, 1, sibling)
+        new[0] = rows.astype(f32).T.astype(bf16)
+        for g in (4, 7, 5, 6, 3, 1, 2):
+            dx, dy = CHIPS[g]
+            back = GROUP_OF[(-dx if abs(dx) == 1 else dx, dy)]
+            go(g, 0, 2 * back, (owner_at(dx, dy, 0), tp))
+        go(0, 0, 1, sibling)
     go_v(1, 0, 2, right)
     go_v(2, 0, 4, left)
     go_k(3, 0, 8, across)
+    score_cached(0, 1, 1)
 
     def choose(pair, carry):
         want = jnp.concatenate(
@@ -202,59 +217,55 @@
 
     lax.fori_loop(0, OWNERS // 2, choose, 0)
 
-    for g in (1, 2, 3, 4, 5, 6, 7):
-        landed_n(2 * g)
-        go_n(7 + g, 2 * g, 2 * g + 1, sibling)
+    def pass_over(go, landed):
+        for g in (1, 2, 3, 4, 5, 6, 7):
+            landed(2 * g)
+            go(7 + g, 2 * g, 2 * g + 1, sibling)
+
+    def picked(new, pair):
+        rows = jnp.concatenate([new[slot] for slot in range(OWNERS)], axis=1)
+        return jnp.dot(rows, hot[pair], preferred_element_type=f32)
+
+    def pick_keys(pair):
+        got = picked(newk, pair)
+        for i in range(2):
+            kn[2 * pair + i] = got[:, i * NEW : (i + 1) * NEW].T.astype(bf16)
+
+    def pick_values(pair):
+        got = picked(newv, pair)
+        for i in range(2):
+            vn[2 * pair + i] = got[:, i * NEW : (i + 1) * NEW].astype(bf16)
+
+    landed_k(1)
+    score_cached(1, 0, 2)
+    pass_over(go_nk, landed_nk)
     go_v(3, 0, 8, across)
     landed_k(2)
     go_k(4, 2, 6, right)
     go_k(5, 2, 3, sibling)
     landed_k(4)
     go_k(6, 4, 5, sibling)
-    landed_n(1)
-    for g in range(1, 8):
-        landed_n(2 * g + 1)
-
-    def pick(pair):
-        rows = jnp.concatenate([newt[slot] for slot in range(OWNERS)], axis=1)
-        got = jnp.dot(rows, hot[pair], preferred_element_type=f32)
-        for i in range(2):
-            cols = slice(i * NEW, (i + 1) * NEW)
-            kn[2 * pair + i] = got[:HEAD_DIM, cols].T.astype(bf16)
-            vn[2 * pair + i] = got[HEAD_DIM:, cols].astype(bf16)
-
-    pick(0)
+    score_cached(1, 1, 3)
+    for g in range(8):
+        landed_nk(2 * g + 1)
+    pick_keys(0)
+    pass_over(go_nv, landed_nv)
     for c in range(SPLITS):
-        s = masked(scores(kn[0], 0, c), 0)
-        sb[CACHE:, columns(c)] = s
-        mb[:, columns(c)] = jnp.maximum(mb[:, columns(c)], peaks(s))
+        score_new(0, 0, 0, c)
     for i in range(SPLITS + 1):
         if i >= 1:
-            score(0, 1, i - 1)
+            score_new(0, 1, 1, i - 1)
         if i < SPLITS:
-            weigh(i)
+            weigh(i, 0)
+    for g in range(8):
+        landed_nv(2 * g + 1)
+    pick_values(0)
 
     def relay(slot):
-        @pl.when(slot % 2 == 1)
-        def _():
-            pick((slot + 1) // 2)
-
-        @pl.when(slot == 0)
-        def _():
-            landed_k(1)
-            landed_v(1)
-
-        @pl.when(slot == 1)
-        def _():
-            landed_v(2)
-            go_v(4, 2, 3, sibling)
-            landed_v(4)
-            go_v(5, 4, 6, left)
-            go_v(6, 4, 5, sibling)
-            landed_k(8)
-            go_k(7, 8, 10, right)
-            go_k(8, 8, 12, left)
-            go_k(9, 8, 9, sibling)
+        @pl.when((slot % 2 == 1) & (slot > 1))
+        def _():
+            pick_keys((slot + 1) // 2)
+            pick_values((slot + 1) // 2)
 
         @pl.when(slot == 2)
         def _():
@@ -316,6 +327,37 @@
             landed_k(15)
             landed_v(15)
 
+    def light_step(j, carry):
+        for i in range(SPLITS + 2):
+            if i >= 2:
+                score_new(1, j, j + 2, i - 2)
+            if 1 <= i <= SPLITS:
+                weigh(i - 1, j + 1)
+            if i < SPLITS:
+                mix(0, j, i)
+        return carry
+
+    lax.fori_loop(0, TILES, light_step, 0)
+    landed_v(1)
+    landed_v(2)
+    go_v(4, 2, 3, sibling)
+    landed_v(4)
+    go_v(5, 4, 6, left)
+    go_v(6, 4, 5, sibling)
+    landed_k(8)
+    go_k(7, 8, 10, right)
+    go_k(8, 8, 12, left)
+    go_k(9, 8, 9, sibling)
+    pick_keys(1)
+    pick_values(1)
+    for i in range(SPLITS + 2):
+        if i >= 2:
+            score(2, 0, i - 2)
+        if 1 <= i <= SPLITS:
+            weigh(i - 1, 3)
+        if i < SPLITS:
+            mix(1, 0, i)
+
     def owner_step(slot, carry):
         relay(slot)
 
@@ -329,9 +371,9 @@
                     mix(slot, j, i)
             return carry
 
-        return lax.fori_loop(0, TILES, step, carry)
-
-    lax.fori_loop(0, OWNERS - 1, owner_step, 0)
+        return lax.fori_loop(jnp.maximum(2 - slot, 0), TILES, step, carry)
+
+    lax.fori_loop(1, OWNERS - 1, owner_step, 0)
     for i in range(SPLITS + 1):
         if i >= 1:
             weigh(i - 1)
@@ -349,7 +391,8 @@
     for d in range(1, TP):
         pltpu.make_async_copy(pack.at[0], pack.at[0], p1_send.at[d - 1]).wait()
     for at in range(15):
-        gone_n(at)
+        gone_nk(at)
+        gone_nv(at)
         gone_k(at)
         gone_v(at)
 
@@ -366,7 +409,8 @@
         scratch_shapes=[
             vmem((OWNERS, CACHE, HEAD_DIM), bf16),
             vmem((OWNERS, HEAD_DIM, CACHE), bf16),
-            vmem((OWNERS, 2 * HEAD_DIM, NEW), bf16),
+            vmem((OWNERS, HEAD_DIM, NEW), bf16),
+            vmem((OWNERS, HEAD_DIM, NEW), bf16),
             vmem((OWNERS, NEW, HEAD_DIM), bf16),
             vmem((OWNERS, HEAD_DIM, NEW), bf16),
             vmem((OWNERS, NEW, NEW), f32),
@@ -375,6 +419,8 @@
             vmem((TP, 32, HEAD_DIM), bf16),
             vmem((TP, 32, HEAD_DIM), bf16),
             vmem((ROWS, 2 * HEAD_DIM), bf16),
+            vmem((AHEAD, CACHE, TILE), f32),
+            vmem((AHEAD, 8, TILE), f32),
             vmem((KEYS, TILE), f32),
             vmem((8, TILE), f32),
             vmem((KEYS, TILE), bf16),
@@ -392,6 +438,8 @@
             dma((OWNERS,)),
             dma((15,)),
             dma((OWNERS,)),
+            dma((15,)),
+            dma((OWNERS,)),
         ],
         compiler_params=pltpu.CompilerParams(
             collective_id=0, has_side_effects=True, vmem_limit_bytes=60 * 2**20

time: 75.5 us -> 73.7 us (0.976)
  Pallas kernels: 73.4 us -> 71.6 us
    pallas_call x1, Pallas kernels: 73.4 us -> 71.6 us  [on_device(): pl.pallas_call(kernel, out_shape=jax.ShapeDtypeStruct(queries.shape, quer...]
where the time goes in v1:
time: 73.7 us; the launch traced here: 73.5 us
  Pallas kernels  71.6 us (97%)
  local copies, waits for them, and re-layouts  1.88 us (3%)
    pallas_call x1, Pallas kernels, on_device(): pl.pallas_call(kernel, out_shape=jax.ShapeDtypeStruct(queries.shape, quer...  71.6 us
    unnamed x1, local copies, waits for them, and re-layouts  1.88 us

profile of v1, /device:TPU:1, one launch (start us, length us, event | category | flops | bytes accessed | tf_op | source)
XLA Modules:
  0.0 73.5 jit_solution(15909830777269090704)
XLA Ops:
  0.0 71.6 %shard_map.64 = bf16[128,2048]{1,0:T(8,128)(2,1)} custom-call(bf16[128,2048]{1,0:T(8,128)(2,1)} %q_ref.1, bf16[1024,128]{1,0:T(8,128)(2,1)} %ck_ref.1, bf16[1024,128]{1,0:T(8,128)(2,1)} %cv_ref.1, bf16[16,1024]{1,0:T(8,128)(2,1)} %nk_ref.1, bf16[16,1024]{1,0:T(8,128)(2,1)} %nv_ref.1, s32[16,128]{1,0:T(8,128)} %bitcast.1), custom_call_target="tpu_custom_call" | custom-call | tf_op jit(solution)/shard_map/pallas_call | solution.py:404
  71.6 1.9 %copy.8 = bf16[128,2048]{1,0:T(8,128)(2,1)} copy(bf16[128,2048]{1,0:T(8,128)(2,1)} %shard_map.64) | data formatting | bytes 1048576

commit v2 on v1

--- a/solution.py
+++ b/solution.py
@@ -32,8 +32,8 @@
 
 
 def kernel(
-    q_ref, ck_ref, cv_ref, nk_ref, nv_ref, src_ref, o_ref,
-    kc, vc, newk, newv, kn, vn, lim, hot, vtmp, pack, stage, q2, sa, ma, sb, mb, pb, lb, mm, acc, den, top,
+    q_in, ck_ref, cv_ref, nk_in, nv_in, src_in, o_ref,
+    q_ref, nk_ref, nv_ref, src_ref, kc, vc, newk, newv, kn, vn, lim, hot, vtmp, pack, stage, q2, sa, ma, sb, mb, pb, lb, mm, acc, den, top,
     local_sem, p1_send, p1_recv, nk_send, nk_recv, nv_send, nv_recv, k_send, k_recv, v_send, v_recv,
 ):
     ctx, tp = lax.axis_index("ctx"), lax.axis_index("tp")
@@ -55,18 +55,19 @@
 
     def remote(src, dst, send, recv, to):
         return pltpu.make_async_remote_copy(
-            src_ref=src, dst_ref=dst, send_sem=send, recv_sem=recv, device_id=to, device_id_type=MESH
+            src_ref=src, dst_ref=dst, send_sem=send.at[0], recv_sem=recv, device_id=to, device_id_type=MESH
         )
 
     def carrier(buf, send, recv):
         def go(at, src, dst, to):
-            remote(buf.at[src], buf.at[dst], send.at[at], recv.at[dst], to).start()
+            remote(buf.at[src], buf.at[dst], send, recv.at[dst], to).start()
 
         def landed(slot):
             pltpu.make_async_copy(buf.at[slot], buf.at[slot], recv.at[slot]).wait()
 
-        def gone(at):
-            pltpu.make_async_copy(buf.at[0], buf.at[0], send.at[at]).wait()
+        def gone():
+            every = buf.at[pl.ds(0, 15)]
+            pltpu.make_async_copy(every, every, send.at[0]).wait()
 
         return go, landed, gone
 
@@ -83,8 +84,16 @@
 
     own_k = pltpu.make_async_copy(ck_ref, kc.at[0], local_sem.at[0])
     own_v = pltpu.make_async_copy(cv_ref, vtmp, local_sem.at[1])
-    own_k.start()
-    own_v.start()
+    fetched = [
+        pltpu.make_async_copy(here, there, local_sem.at[2 + i])
+        for i, (here, there) in enumerate(
+            ((nk_in, nk_ref), (nv_in, nv_ref), (q_in, q_ref), (src_in, src_ref))
+        )
+    ]
+    for copy in fetched[:2] + [own_k, own_v] + fetched[2:]:
+        copy.start()
+    for copy in fetched[:2]:
+        copy.wait()
     for h in range(TP):
         cols = slice(h * HEAD_DIM, (h + 1) * HEAD_DIM)
         pack[h, :16, :] = nk_ref[:, cols]
@@ -95,11 +104,13 @@
     pl.semaphore_wait(barrier, len(peers))
     for d in range(1, TP):
         head = (tp + d) % TP
-        remote(pack.at[head], stage.at[tp], p1_send.at[d - 1], p1_recv.at[d - 1], (ctx, head)).start()
+        remote(pack.at[head], stage.at[tp], p1_send, p1_recv.at[d - 1], (ctx, head)).start()
     go_k(0, 0, 1, sibling)
     go_k(1, 0, 2, right)
     go_k(2, 0, 4, left)
 
+    for copy in fetched[2:]:
+        copy.wait()
     for h in range(GROUP):
         rows = pl.ds(h * NEW, NEW)
         part = q_ref[:, pl.ds(h * HEAD_DIM, HEAD_DIM)].astype(f32) * SCALE
@@ -222,19 +233,27 @@
             landed(2 * g)
             go(7 + g, 2 * g, 2 * g + 1, sibling)
 
-    def picked(new, pair):
-        rows = jnp.concatenate([new[slot] for slot in range(OWNERS)], axis=1)
+    def everyone(new):
+        return jnp.concatenate([new[slot] for slot in range(OWNERS)], axis=1)
+
+    def picked(rows, pair):
         return jnp.dot(rows, hot[pair], preferred_element_type=f32)
 
     def pick_keys(pair):
-        got = picked(newk, pair)
+        got = picked(everyone(newk), pair)
         for i in range(2):
             kn[2 * pair + i] = got[:, i * NEW : (i + 1) * NEW].T.astype(bf16)
 
     def pick_values(pair):
-        got = picked(newv, pair)
+        got = picked(everyone(newv), pair)
         for i in range(2):
             vn[2 * pair + i] = got[:, i * NEW : (i + 1) * NEW].astype(bf16)
+
+    def pick(pair):
+        got = picked(jnp.concatenate([everyone(newk), everyone(newv)], axis=0), pair)
+        for i in range(2):
+            kn[2 * pair + i] = got[:HEAD_DIM, i * NEW : (i + 1) * NEW].T.astype(bf16)
+            vn[2 * pair + i] = got[HEAD_DIM:, i * NEW : (i + 1) * NEW].astype(bf16)
 
     landed_k(1)
     score_cached(1, 0, 2)
@@ -264,8 +283,7 @@
     def relay(slot):
         @pl.when((slot % 2 == 1) & (slot > 1))
         def _():
-            pick_keys((slot + 1) // 2)
-            pick_values((slot + 1) // 2)
+            pick((slot + 1) // 2)
 
         @pl.when(slot == 2)
         def _():
@@ -274,9 +292,6 @@
         @pl.when(slot == 3)
         def _():
             landed_v(3)
-            landed_k(6)
-            go_k(10, 6, 14, across)
-            go_k(11, 6, 7, sibling)
             landed_v(8)
             go_v(7, 8, 10, right)
             go_v(8, 8, 12, left)
@@ -286,13 +301,19 @@
         def _():
             landed_k(5)
             landed_v(5)
+            landed_k(6)
+            go_k(10, 6, 14, across)
+            go_k(11, 6, 7, sibling)
+
+        @pl.when(slot == 6)
+        def _():
+            landed_k(7)
             landed_v(6)
             go_v(10, 6, 14, across)
             go_v(11, 6, 7, sibling)
 
-        @pl.when(slot == 6)
-        def _():
-            landed_k(7)
+        @pl.when(slot == 7)
+        def _():
             landed_v(7)
             landed_k(10)
             go_k(12, 10, 11, sibling)
@@ -303,18 +324,24 @@
         def _():
             landed_k(9)
             landed_v(9)
+
+        @pl.when(slot == 9)
+        def _():
             landed_v(10)
             go_v(12, 10, 11, sibling)
             landed_v(12)
             go_v(13, 12, 13, sibling)
+
+        @pl.when(slot == 10)
+        def _():
+            landed_k(11)
             landed_k(14)
             go_k(14, 14, 15, sibling)
             landed_v(14)
             go_v(14, 14, 15, sibling)
 
-        @pl.when(slot == 10)
-        def _():
-            landed_k(11)
+        @pl.when(slot == 11)
+        def _():
             landed_v(11)
 
         @pl.when(slot == 12)
@@ -348,8 +375,7 @@
     go_k(7, 8, 10, right)
     go_k(8, 8, 12, left)
     go_k(9, 8, 9, sibling)
-    pick_keys(1)
-    pick_values(1)
+    pick(1)
     for i in range(SPLITS + 2):
         if i >= 2:
             score(2, 0, i - 2)
@@ -388,13 +414,12 @@
         part = acc[j, :, at : at + NEW] * (1.0 / den[j, :, at : at + NEW])
         o_ref[:, h * HEAD_DIM : (h + 1) * HEAD_DIM] = part.T.astype(bf16)
 
-    for d in range(1, TP):
-        pltpu.make_async_copy(pack.at[0], pack.at[0], p1_send.at[d - 1]).wait()
-    for at in range(15):
-        gone_nk(at)
-        gone_nv(at)
-        gone_k(at)
-        gone_v(at)
+    packs = pack.at[pl.ds(0, TP - 1)]
+    pltpu.make_async_copy(packs, packs, p1_send.at[0]).wait()
+    gone_nk()
+    gone_nv()
+    gone_k()
+    gone_v()
 
 
 def on_device(queries, cache_keys, cache_values, new_keys, new_values, sources):
@@ -404,9 +429,13 @@
     return pl.pallas_call(
         kernel,
         out_shape=jax.ShapeDtypeStruct(queries.shape, queries.dtype),
-        in_specs=[whole, there, there, whole, whole, whole],
+        in_specs=[there] * 6,
         out_specs=whole,
         scratch_shapes=[
+            vmem(queries.shape, bf16),
+            vmem(new_keys.shape, bf16),
+            vmem(new_values.shape, bf16),
+            vmem((OWNERS, NEW), jnp.int32),
             vmem((OWNERS, CACHE, HEAD_DIM), bf16),
             vmem((OWNERS, HEAD_DIM, CACHE), bf16),
             vmem((OWNERS, HEAD_DIM, NEW), bf16),
@@ -429,16 +458,16 @@
             vmem((TILES, HEAD_DIM, TILE), f32),
             vmem((TILES, 1, TILE), f32),
             vmem((TILES, 1, TILE), f32),
-            dma((2,)),
+            dma((6,)),
+            dma((1,)),
             dma((7,)),
-            dma((7,)),
-            dma((15,)),
+            dma((1,)),
             dma((OWNERS,)),
-            dma((15,)),
+            dma((1,)),
             dma((OWNERS,)),
-            dma((15,)),
+            dma((1,)),
             dma((OWNERS,)),
-            dma((15,)),
+            dma((1,)),
             dma((OWNERS,)),
         ],
         compiler_params=pltpu.CompilerParams(

time: 73.7 us -> 73.3 us (level)
  no operation moved by 1% of the time
where the time goes in v2:
time: 73.3 us; the launch traced here: 73.2 us
  Pallas kernels  71.3 us (97%)
  local copies, waits for them, and re-layouts  1.88 us (3%)
    pallas_call x1, Pallas kernels, on_device(): pl.pallas_call(kernel, out_shape=jax.ShapeDtypeStruct(queries.shape, quer...  71.3 us
    unnamed x1, local copies, waits for them, and re-layouts  1.88 us

profile of v2, /device:TPU:1, one launch (start us, length us, event | category | flops | bytes accessed | tf_op | source)
XLA Modules:
  0.0 73.2 jit_solution(9103732787858679682)
XLA Ops:
  0.0 71.3 %shard_map.64 = bf16[128,2048]{1,0:T(8,128)(2,1)} custom-call(bf16[128,2048]{1,0:T(8,128)(2,1)} %q_in.1, bf16[1024,128]{1,0:T(8,128)(2,1)} %ck_ref.1, bf16[1024,128]{1,0:T(8,128)(2,1)} %cv_ref.1, bf16[16,1024]{1,0:T(8,128)(2,1)} %nk_in.1, bf16[16,1024]{1,0:T(8,128)(2,1)} %nv_in.1, s32[16,128]{1,0:T(8,128)} %bitcast.1), custom_call_target="tpu_custom_call" | custom-call | tf_op jit(solution)/shard_map/pallas_call | solution.py:429
  71.3 1.9 %copy.8 = bf16[128,2048]{1,0:T(8,128)(2,1)} copy(bf16[128,2048]{1,0:T(8,128)(2,1)} %shard_map.64) | data formatting | bytes 1048576
